TPU v7x, 256 devices: a whole 4x4x8 slice. The times are simulated.
256 devices in a mesh: teacher: 8 (over z_hi, x), seq: 32 (over y, z_lo, core).
Axes of the slice: x: 4, y: 4, z: 8 (z_hi: 2, z_lo: 4; z = z_hi * 4 + z_lo), core: 2. Of those that a mesh axis runs over, the one named last changes fastest.
Arguments:
- tokens: bfloat16 [16384, 2048], P(('teacher', 'seq')), may hold values from -6 to 6
- router_weight: bfloat16 [2048, 64], replicated, may hold values from -0.25 to 0.25
- gate_weight: bfloat16 [64, 1536, 2048], P('seq', 'teacher'), may hold values from -0.125 to 0.125
- up_weight: bfloat16 [64, 1536, 2048], P('seq', 'teacher'), may hold values from -0.125 to 0.125
- down_weight: bfloat16 [64, 1536, 2048], P('seq', 'teacher'), may hold values from -0.15625 to 0.15625
- routing: int32 [16384, 2], P(('teacher', 'seq')), may hold values from 0 to 63, all different within a row; in each aligned block of 64 rows (0 to 63, 64 to 127, ...) at most 3 rows name the same one
- lengths: int32 [64], replicated, may hold values from 128 to 256, as said below
Outputs:
- mixed: bfloat16 [16384, 2048], P(('teacher', 'seq'))
Inputs may be any that keep to these rules, and one draw needn't show every extreme that they name: `routing`: within the 64 rows of one device no expert is named more than 3 times, and in every draw some expert is named exactly 3 times there. `lengths`: some response window is fully live, 256 tokens.
All inputs are finite; a program needn't handle non-finite values.
Results may differ from a plain program's by a relative error of at most 0.017.
Values may be sent and summed in bfloat16 or wider, within the bound.
A program may use at most 64 MiB of HBM per device.

v0:
```python
import jax
import jax.numpy as jnp
from jax import lax
from jax.sharding import PartitionSpec as P


def normalize(tokens):
    values = tokens.astype(jnp.float32)
    scale = lax.rsqrt(jnp.mean(values * values, axis=-1, keepdims=True) + 1e-06)
    return (values * scale).astype(jnp.bfloat16)


def expert_mlp(segment, gate_weight, up_weight, down_weight):
    gate = jnp.einsum("erd,efd->erf", segment, gate_weight, preferred_element_type=jnp.float32)
    upper = jnp.einsum("erd,efd->erf", segment, up_weight, preferred_element_type=jnp.float32)
    hidden = (jax.nn.silu(gate) * upper).astype(jnp.bfloat16)
    return jnp.einsum(
        "erf,efd->erd", hidden, down_weight, preferred_element_type=jnp.float32
    ).astype(jnp.bfloat16)


def plan_routes(
    normed, router_weight, routing, lengths, block_index, length_all, experts, capacity
):
    tok_dev = normed.shape[0]
    top_count = routing.shape[1]
    logits = jnp.dot(normed, router_weight, preferred_element_type=jnp.float32)
    chosen = jnp.take_along_axis(logits, routing, axis=1)
    scores = jax.nn.sigmoid(chosen)
    position = block_index * tok_dev + jnp.arange(tok_dev, dtype=jnp.int32)
    response = position // length_all
    offset = position - response * length_all
    limit = jnp.sum(
        jnp.where(
            response[:, None] == jnp.arange(lengths.shape[0], dtype=jnp.int32)[None, :],
            lengths[None, :],
            0,
        ),
        axis=1,
    )
    is_live = offset < limit
    route_weight = jnp.where(
        is_live[:, None],
        scores / jnp.sum(scores, axis=1, keepdims=True),
        jnp.zeros((), jnp.float32),
    )
    flat_ids = routing.reshape(-1)
    flat_live = jnp.repeat(is_live, top_count)
    onehot = (
        (flat_ids[:, None] == jnp.arange(experts, dtype=jnp.int32)[None, :]) & flat_live[:, None]
    ).astype(jnp.int32)
    ranking = jnp.cumsum(onehot, axis=0) - onehot
    slot_ids = jnp.sum(ranking * onehot, axis=1)
    target = jnp.where(flat_live, flat_ids * capacity + slot_ids, -1).reshape(tok_dev, top_count)
    return (target, route_weight)


def local(tokens, router_weight, gate_weight, up_weight, down_weight, routing, lengths):
    tok_dev = tokens.shape[0]
    top_count = routing.shape[1]
    width = tokens.shape[1]
    seq_size = lax.axis_size("seq")
    group_size = lax.axis_size("teacher")
    experts = gate_weight.shape[0] * seq_size
    capacity = max(2, tok_dev * top_count // experts + 1)
    slots_all = experts * capacity
    length_all = 4 * tok_dev
    block_index = lax.axis_index("teacher") * seq_size + lax.axis_index("seq")
    normed = normalize(tokens)
    target, route_weight = plan_routes(
        normed, router_weight, routing, lengths, block_index, length_all, experts, capacity
    )
    gathered_rows, gathered_target = (
        lax.all_gather(normed, "teacher", axis=0, tiled=True),
        lax.all_gather(target, "teacher", axis=0, tiled=True),
    )
    grouped_target = gathered_target.reshape(group_size, tok_dev, top_count)
    select = jnp.any(
        grouped_target[:, None, :, :]
        == jnp.arange(slots_all, dtype=jnp.int32)[None, :, None, None],
        axis=-1,
    )
    select = select.astype(jnp.bfloat16).reshape(group_size, experts, capacity, tok_dev)
    dispatched = jnp.einsum(
        "bect,btd->ebcd",
        select,
        gathered_rows.reshape(group_size, tok_dev, width),
        preferred_element_type=jnp.float32,
    ).astype(jnp.bfloat16)
    segment = lax.all_to_all(dispatched, "seq", split_axis=0, concat_axis=2, tiled=True)
    shaped = segment.reshape(segment.shape[0], -1, segment.shape[-1])
    partials = expert_mlp(shaped, gate_weight, up_weight, down_weight).reshape(segment.shape)
    returned = lax.all_to_all(partials, "seq", split_axis=2, concat_axis=0, tiled=True)
    summed = lax.psum_scatter(
        returned.astype(jnp.float32).astype(jnp.bfloat16),
        "teacher",
        scatter_dimension=1,
        tiled=True,
    ).astype(jnp.float32)
    expert_out = summed.reshape(slots_all, width).astype(jnp.bfloat16)
    picked = jnp.take(expert_out, jnp.maximum(target, 0).reshape(-1), axis=0).reshape(
        tok_dev, top_count, width
    )
    mixed = jnp.sum(picked.astype(jnp.float32) * route_weight[:, :, None], axis=1)
    return mixed.astype(jnp.bfloat16)


def solution(mesh):
    in_specs = (
        P(("teacher", "seq"), None),
        P(),
        P("seq", "teacher", None),
        P("seq", "teacher", None),
        P("seq", "teacher", None),
        P(("teacher", "seq"), None),
        P(),
    )
    out_specs = P(("teacher", "seq"), None)
    return jax.shard_map(local, mesh=mesh, in_specs=in_specs, out_specs=out_specs, check_vma=False)
```

profile of v0, /device:TPU:1, one launch (start us, length us, event | category | flops | bytes accessed | tf_op | source)
XLA Modules:
  0.0 598.3 jit_solution(16673362132184829474)
XLA Ops:
  6.5 1.2 fusion.18
  7.8 1.8 fusion.19
  9.6 0.8 select_reduce_fusion.1
  10.6 0.2 and.43
  10.7 0.8 copy.122
  11.8 0.2 reduce_window_sum.11
  11.9 0.2 select_reduce_fusion
  12.3 0.7 broadcast_compare_fusion
  13.0 29.3 %all-gather = s32[8,64,2]{1,2,0:T(2,128)S(1)} all-gather(s32[1,64,2]{1,2,0:T(2,128)S(1)} %bitcast.40), channel_id=1, replica_groups=mesh['teacher'=8,'seq'=32] {'teacher'}, dimensions={0}, use_global_device_ids=true | all-gather | bytes 4608 | tf_op jit(solution)/shard_map/all_gather | solution.py:75
  42.4 0.2 fusion.15
  42.6 0.4 copy.126
  43.0 45.8 %all-gather.3.cloned.1.call-done = bf16[512,2048]{1,0:T(8,128)(2,1)} async-done(((bf16[64,2048]{1,0:T(8,128)(2,1)}), bf16[512,2048]{1,0:T(8,128)(2,1)}) %all-gather.3.cloned.1.call-update) | async-done | bytes 2097168 | tf_op jit(solution)/shard_map/all_gather | solution.py:74
  88.7 3.4 convert_bitcast_fusion
  92.1 3.4 copy.128
  95.6 146.4 %all_to_all.33 = bf16[64,8,3,2048]{3,1,2,0:T(8,128)(2,1)S(1)} all-to-all(bf16[64,8,3,2048]{3,1,2,0:T(8,128)(2,1)S(1)} %copy.128), channel_id=1, replica_groups=mesh['teacher'=8,'seq'=32] {'seq'}, dimensions={0} | all-to-all | bytes 12582912 | tf_op jit(solution)/shard_map/all_to_all | solution.py:90
  242.0 13.9 %copy.129 = bf16[32,2,8,3,2048]{4,1,3,0,2:T(2,128)(2,1)S(1)} copy(bf16[32,2,8,3,2048]{4,2,3,1,0:T(8,128)(2,1)S(1)} %bitcast.32) | data formatting | bytes 12582912 | tf_op jit(solution)/shard_map/all_to_all | solution.py:90
  255.9 2.7 copy-done.2
  258.5 5.4 fusion.2
  263.9 15.3 %convolution_convert_fusion = bf16[2,768,2048]{2,1,0:T(8,128)(2,1)} fusion(bf16[2,192,2048]{2,1,0:T(8,128)(2,1)S(1)} %copy-done, bf16[2,192,2048]{2,1,0:T(8,128)(2,1)S(1)} %copy-done.7, bf16[2,768,2048]{2,0,1:T(2,128)(2,1)} %bitcast.36, f32[2,768,192]{1,2,0:T(8,128)} %fusion.2), kind=kOutput, calls=%fused_computation.7 | convolution fusion | flops 2420834304 | bytes 16908288 | tf_op jit(solution)/shard_map/erf,efd->erd/dot_general | solution.py:17
  279.2 6.2 %copy.132 = bf16[2,8,96,2048]{3,1,0,2:T(8,128)(2,1)S(1)} copy(bf16[2,8,96,2048]{3,2,1,0:T(8,128)(2,1)} %bitcast.37) | data formatting | bytes 12582912 | tf_op jit(solution)/shard_map/reshape | solution.py:92
  285.5 143.9 %all_to_all.34 = bf16[2,8,96,2048]{3,1,0,2:T(8,128)(2,1)S(1)} all-to-all(bf16[2,8,96,2048]{3,1,0,2:T(8,128)(2,1)S(1)} %copy.132), channel_id=1, replica_groups=mesh['teacher'=8,'seq'=32] {'seq'}, dimensions={2} | all-to-all | bytes 12582912 | tf_op jit(solution)/shard_map/all_to_all | solution.py:93
  429.3 1.1 copy.134
  430.5 6.1 %copy.135 = bf16[64,8,3,2048]{3,0,2,1:T(8,128)(2,1)} copy(bf16[64,8,3,2048]{3,1,2,0:T(8,128)(2,1)S(1)} %bitcast.34) | data formatting | bytes 12582912 | tf_op jit(solution)/shard_map/all_to_all | solution.py:93
  436.6 0.6 copy-done.5
  437.9 0.2 fusion.25
  438.1 1.3 gather_fusion.1
  439.8 144.7 %reduce-scatter.2.cloned.1.call-done = bf16[64,1,3,2048]{3,0,2,1:T(8,128)(2,1)} async-done(((bf16[64,8,3,2048]{3,0,2,1:T(8,128)(2,1)}), bf16[64,1,3,2048]{3,0,2,1:T(8,128)(2,1)}) %reduce-scatter.2.cloned.1.call-update) | async-done | bytes 786448 | tf_op jit(solution)/shard_map/reduce_scatter | solution.py:94
  584.5 1.8 copy.136
  586.3 0.7 convert_element_type.42
  587.0 0.9 gather_fusion
  587.9 0.3 gather.11
  588.3 3.2 multiply_reduce_fusion
  (40 shorter events, 1.6 us)
Async XLA Ops:
  6.5 257.4 %copy-start = (bf16[2,192,2048]{2,1,0:T(8,128)(2,1)S(1)}, bf16[2,192,2048]{2,1,0:T(8,128)(2,1)}, u32[]{:S(2)}) copy-start(bf16[2,192,2048]{2,1,0:T(8,128)(2,1)} %param.11) | copy-start | bytes 4718596
  6.5 82.2 %all-gather.3.cloned.1.call-start = ((), (), s32[]{:S(2)}) async-start(), calls=%async_computation.3 | async-start | bytes 2359296 | tf_op jit(solution)/shard_map/all_gather | solution.py:74
  9.6 574.9 %reduce-scatter.2.cloned.1.call-start = ((), (), s32[]{:S(2)}) async-start(), calls=%async_computation.4 | async-start | bytes 7077888 | tf_op jit(solution)/shard_map/reduce_scatter | solution.py:94
  242.0 16.5 %copy-start.6 = (bf16[2,192,2048]{2,1,0:T(8,128)(2,1)S(1)}, bf16[2,192,2048]{2,1,0:T(8,128)(2,1)}, u32[]{:S(2)}) copy-start(bf16[2,192,2048]{2,1,0:T(8,128)(2,1)} %param.9) | copy-start | bytes 4718596
  255.9 2.7 copy-start.2
  258.5 5.4 copy-start.7
  436.6 0.7 copy-start.5
  436.6 1.3 copy-start.3
  436.6 1.3 copy-start.4
  587.0 4.5 copy-start.1
Sparse Core Ops, SparseCore 0:
  10.0 78.7 all-gather.2
  436.7 147.6 reduce-scatter.1
where the time goes:
time: 599 us; the launch traced here: 598 us
  blocking collectives  320 us (53%)
  waiting for transfers between devices  191 us (32%)
  local copies, waits for them, and re-layouts  41.7 us (7%)
  matrix products  24.3 us (4%)
  between operations  13.6 us (2%)
  other arithmetic  8.46 us (1%)
    all_to_all x1, blocking collectives, local(): lax.all_to_all(dispatched, 'seq', split_axis=0, concat_axis=2, tiled=True)  146 us
    reduce_scatter x1, waiting for transfers between devices, local(): lax.psum_scatter(returned.astype(jnp.float32).astype(jnp.bfloat16), 'teac...  145 us
    all_to_all x1, blocking collectives, local(): lax.all_to_all(partials, 'seq', split_axis=2, concat_axis=0, tiled=True)  144 us
    all_gather x1, waiting for transfers between devices, local(): lax.all_gather(normed, 'teacher', axis=0, tiled=True)  45.8 us
    all_gather x1, blocking collectives, local(): lax.all_gather(target, 'teacher', axis=0, tiled=True)  29.3 us
    dot_general x1, matrix products, expert_mlp(): jnp.einsum('erf,efd->erd', hidden, down_weight, preferred_element_type=jn...  15.3 us
    all_to_all x1, local copies, waits for them, and re-layouts, local(): lax.all_to_all(dispatched, 'seq', split_axis=0, concat_axis=2, tiled=True)  13.9 us
  transfers between devices with their start and end apart: 2, of which 2 were waited for; matrix products, arithmetic and copies ran while one was open for 1% of the time, Pallas kernels for 0%

commit v1 on v0

v1 whole, which is shorter than its diff:
```python
import functools

import jax
import jax.numpy as jnp
from jax import lax
from jax.experimental import pallas as pl
from jax.experimental.pallas import tpu as pltpu
from jax.sharding import PartitionSpec as P

MESH = pl.DeviceIdType.MESH
NX, NY, NZ, NLO = 4, 4, 8, 4
CHIPS = NX * NY * NZ
LANE = 128
SUB = 16


def normalize(tokens):
    values = tokens.astype(jnp.float32)
    scale = lax.rsqrt(jnp.mean(values * values, axis=-1, keepdims=True) + 1e-06)
    return (values * scale).astype(jnp.bfloat16)


def plan_routes(
    normed, router_weight, routing, lengths, block_index, length_all, experts, capacity
):
    tok_dev = normed.shape[0]
    top_count = routing.shape[1]
    logits = jnp.dot(normed, router_weight, preferred_element_type=jnp.float32)
    expert_ids = jnp.arange(experts, dtype=jnp.int32)
    named = routing[:, :, None] == expert_ids[None, None, :]
    chosen = jnp.sum(jnp.where(named, logits[:, None, :], 0.0), axis=2)
    scores = jax.nn.sigmoid(chosen)
    position = block_index * tok_dev + jnp.arange(tok_dev, dtype=jnp.int32)
    response = position // length_all
    offset = position - response * length_all
    limit = jnp.sum(
        jnp.where(
            response[:, None] == jnp.arange(lengths.shape[0], dtype=jnp.int32)[None, :],
            lengths[None, :],
            0,
        ),
        axis=1,
    )
    is_live = offset < limit
    route_weight = jnp.where(
        is_live[:, None],
        scores / jnp.sum(scores, axis=1, keepdims=True),
        jnp.zeros((), jnp.float32),
    )
    hits = jnp.any(named, axis=1) & is_live[:, None]
    earlier = jnp.arange(tok_dev)[:, None] > jnp.arange(tok_dev)[None, :]
    rank = jnp.dot(
        earlier.astype(jnp.bfloat16), hits.astype(jnp.bfloat16),
        preferred_element_type=jnp.float32,
    ).astype(jnp.int32)
    slot_ids = jnp.sum(jnp.where(named, rank[:, None, :], 0), axis=2)
    target = jnp.where(is_live[:, None], routing * capacity + slot_ids, -1)
    flat = target.reshape(-1)
    owner = jnp.arange(tok_dev * top_count, dtype=jnp.int32) // top_count
    slots = jnp.arange(experts * capacity, dtype=jnp.int32)
    table = jnp.sum(jnp.where(flat[None, :] == slots[:, None], owner[None, :], 0), axis=1)
    return table, jnp.maximum(flat, 0), route_weight.reshape(-1)


def place(sid):
    return sid % NX, sid // (NX * NZ), (sid // NX) % NZ


def device(x, y, z, core):
    return ((z // NLO) * NX + x, (y * NLO + z % NLO) * 2 + core)


def kernel(
    table_ref, target_ref, weight_ref, tok_ref, gate_ref, up_ref, down_ref, out_ref,
    send, recv, rows_in, wbuf, hidden, stage, rsend, back,
    w_send, w_recv, f_send, f_recv, t_send, t_recv, r_send, r_recv,
):
    teacher, seq = lax.axis_index("teacher"), lax.axis_index("seq")
    x, z_hi = teacher % NX, teacher // NX
    core, z_lo, y = seq % 2, (seq // 2) % NLO, seq // (2 * NLO)
    z = z_hi * NLO + z_lo
    me = (y * NZ + z) * NX + x
    my_expert = (y * NLO + z_lo) * NX + x
    depth = gate_ref.shape[1]
    half = depth // 2
    cap = send.shape[1]
    chunk_src = CHIPS // NY
    chunk_rows = chunk_src * cap

    barrier = pltpu.get_barrier_semaphore()

    @pl.loop(1, CHIPS)
    def _(i):
        px, py, pz = place((me + i) % CHIPS)
        pl.semaphore_signal(
            barrier, inc=1, device_id=device(px, py, pz, core), device_id_type=MESH
        )

    for px in range(NX):
        pl.semaphore_signal(
            barrier, inc=1, device_id=device(px, y, z, 1 - core), device_id_type=MESH
        )
    pl.semaphore_wait(barrier, CHIPS - 1 + NX)

    weights = (gate_ref, up_ref, down_ref)
    for i in range(2):
        goal = 2 * core + i

        @pl.when(goal != x)
        def _():
            for part in range(2):
                for m in range(3):
                    pltpu.make_async_remote_copy(
                        src_ref=weights[m].at[i, pl.ds(part * half, half), :],
                        dst_ref=wbuf.at[x, m, pl.ds(part * half, half), :],
                        send_sem=w_send,
                        recv_sem=w_recv.at[x],
                        device_id=device(goal, y, z, part),
                        device_id_type=MESH,
                    ).start()

        @pl.when(goal == x)
        def _():
            for m in range(3):
                pltpu.make_async_copy(weights[m].at[i], wbuf.at[x, m], w_recv.at[x]).start()
                pltpu.make_async_remote_copy(
                    src_ref=weights[m].at[i],
                    dst_ref=wbuf.at[x, m],
                    send_sem=w_send,
                    recv_sem=w_recv.at[x],
                    device_id=device(x, y, z, 1 - core),
                    device_id_type=MESH,
                ).start()

    experts = send.shape[0]

    @pl.loop(0, experts)
    def _(e):
        for r in range(cap):
            send[e, r] = tok_ref[table_ref[e * cap + r]]

    pltpu.make_async_copy(send.at[my_expert], recv.at[me], t_recv).start()

    @pl.loop(1, CHIPS)
    def _(i):
        px, py, pz = place((me + i) % CHIPS)
        pltpu.make_async_remote_copy(
            src_ref=send.at[(py * NLO + pz % NLO) * NX + px],
            dst_ref=recv.at[me],
            send_sem=t_send,
            recv_sem=t_recv,
            device_id=device(px, py, pz, core),
            device_id_type=MESH,
        ).start()

    def half_of(s, part):
        return wbuf.at[s, :, pl.ds(part * half, half), :]

    def forward(d):
        s = (x + d) % NX
        mine = half_of(s, core)
        pltpu.make_async_copy(mine, mine, w_recv.at[s]).wait()
        pltpu.make_async_remote_copy(
            src_ref=mine,
            dst_ref=mine,
            send_sem=f_send.at[s],
            recv_sem=f_recv.at[s],
            device_id=device(x, y, z, 1 - core),
            device_id_type=MESH,
        ).start()

    def first_layer(d):
        s = (x + d) % NX
        if d == 0:
            pltpu.make_async_copy(wbuf.at[s], wbuf.at[s], w_recv.at[s]).wait()
        else:
            other = half_of(s, 1 - core)
            pltpu.make_async_copy(other, other, f_recv.at[s]).wait()

        @pl.loop(0, rows_in.shape[0] // 128)
        def _(b):
            at = pl.ds(pl.multiple_of(b * 128, 128), 128)
            block = rows_in[at, :]
            dims = (((1,), (1,)), ((), ()))
            gate = lax.dot_general(block, wbuf[s, 0], dims, preferred_element_type=jnp.float32)
            upper = lax.dot_general(block, wbuf[s, 1], dims, preferred_element_type=jnp.float32)
            hidden[s, at, :] = (gate / (1.0 + jnp.exp(-gate)) * upper).astype(jnp.bfloat16)

    forward(1)
    forward(3)

    pltpu.make_async_copy(recv, recv, t_recv).wait()

    @pl.loop(0, NY)
    def _(g):
        part = recv[pl.ds(g * chunk_src, chunk_src)]
        stage[...] = part.reshape(chunk_rows * SUB, LANE).astype(jnp.float32)
        at = pl.ds(pl.multiple_of(g * chunk_rows, chunk_rows), chunk_rows)
        for k in range(SUB):
            rows_in[at, k * LANE:(k + 1) * LANE] = stage[
                pl.ds(k, chunk_rows, stride=SUB), :
            ].astype(jnp.bfloat16)

    first_layer(0)
    first_layer(1)
    first_layer(3)
    forward(2)
    first_layer(2)

    @pl.loop(0, NY)
    def _(i):
        g = (y + i) % NY
        at = pl.ds(pl.multiple_of(g * chunk_rows, chunk_rows), chunk_rows)
        wide = 512
        for n in range(SUB * LANE // wide):
            total = jnp.zeros((chunk_rows, wide), jnp.float32)
            for s in range(NX):
                total += jnp.dot(
                    hidden[s, at, :], wbuf[s, 2, :, n * wide:(n + 1) * wide],
                    preferred_element_type=jnp.float32,
                )
            for k in range(wide // LANE):
                stage[pl.ds(n * (wide // LANE) + k, chunk_rows, stride=SUB), :] = total[
                    :, k * LANE:(k + 1) * LANE
                ]
        rsend[pl.ds(g * chunk_src, chunk_src)] = (
            stage[...].astype(jnp.bfloat16).reshape(chunk_src, cap, SUB, LANE)
        )

        @pl.loop(0, chunk_src)
        def _(j):
            sid = g * chunk_src + (me + j) % chunk_src
            px, py, pz = place(sid)

            @pl.when(sid != me)
            def _():
                pltpu.make_async_remote_copy(
                    src_ref=rsend.at[sid],
                    dst_ref=back.at[z_hi, my_expert],
                    send_sem=r_send,
                    recv_sem=r_recv,
                    device_id=device(px, py, pz, core),
                    device_id_type=MESH,
                ).start()

            @pl.when(sid == me)
            def _():
                pltpu.make_async_copy(rsend.at[sid], back.at[z_hi, my_expert], r_recv).start()

    pltpu.make_async_copy(back, back, r_recv).wait()

    tokens = tok_ref.shape[0]

    @pl.loop(0, tokens)
    def _(t):
        total = jnp.zeros((SUB, LANE), jnp.float32)
        for k in range(2):
            slot = target_ref[2 * t + k]
            e, r = slot // cap, slot % cap
            total += weight_ref[2 * t + k] * (
                back[0, e, r].astype(jnp.float32) + back[1, e, r].astype(jnp.float32)
            )
        out_ref[t] = total.astype(jnp.bfloat16)

    others = pl.ds(0, CHIPS - 1)
    pltpu.make_async_copy(recv.at[others], recv.at[others], t_send).wait()
    pltpu.make_async_copy(rsend.at[others], rsend.at[others], r_send).wait()
    two = pl.ds(0, 2)
    pltpu.make_async_copy(wbuf.at[two], wbuf.at[two], w_send).wait()
    for d in range(1, NX):
        s = (x + d) % NX
        mine = half_of(s, core)
        pltpu.make_async_copy(mine, mine, f_send.at[s]).wait()


def local(tokens, router_weight, gate_weight, up_weight, down_weight, routing, lengths):
    tok_dev, width = tokens.shape
    top_count = routing.shape[1]
    seq_size = lax.axis_size("seq")
    experts = gate_weight.shape[0] * seq_size
    depth = gate_weight.shape[1]
    capacity = max(2, tok_dev * top_count // experts + 1)
    length_all = 4 * tok_dev
    block_index = lax.axis_index("teacher") * seq_size + lax.axis_index("seq")
    normed = normalize(tokens)
    table, target, route_weight = plan_routes(
        normed, router_weight, routing, lengths, block_index, length_all, experts, capacity
    )
    rows = CHIPS * capacity
    smem = pl.BlockSpec(memory_space=pltpu.SMEM)
    vmem = pl.BlockSpec(memory_space=pltpu.VMEM)
    hbm = pl.BlockSpec(memory_space=pl.ANY)
    sem = pltpu.SemaphoreType.DMA
    bf16 = jnp.bfloat16
    mixed = pl.pallas_call(
        kernel,
        out_shape=jax.ShapeDtypeStruct((tok_dev, SUB, LANE), bf16),
        in_specs=[smem, smem, smem, vmem, hbm, hbm, hbm],
        out_specs=vmem,
        scratch_shapes=[
            pltpu.VMEM((experts, capacity, SUB, LANE), bf16),
            pltpu.VMEM((CHIPS, capacity, SUB, LANE), bf16),
            pltpu.VMEM((rows, width), bf16),
            pltpu.VMEM((NX, 3, depth, width), bf16),
            pltpu.VMEM((NX, rows, depth), bf16),
            pltpu.VMEM((rows // NY * SUB, LANE), jnp.float32),
            pltpu.VMEM((CHIPS, capacity, SUB, LANE), bf16),
            pltpu.VMEM((2, experts, capacity, SUB, LANE), bf16),
            sem, sem((NX,)), sem((NX,)), sem((NX,)), sem, sem, sem, sem,
        ],
        compiler_params=pltpu.CompilerParams(
            collective_id=0, has_side_effects=True, vmem_limit_bytes=48 * 1024 * 1024
        ),
    )(
        table, target, route_weight, normed.reshape(tok_dev, SUB, LANE),
        gate_weight, up_weight, down_weight,
    )
    return mixed.reshape(tok_dev, width)


def solution(mesh):
    in_specs = (
        P(("teacher", "seq"), None),
        P(),
        P("seq", "teacher", None),
        P("seq", "teacher", None),
        P("seq", "teacher", None),
        P(("teacher", "seq"), None),
        P(),
    )
    out_specs = P(("teacher", "seq"), None)
    return jax.shard_map(local, mesh=mesh, in_specs=in_specs, out_specs=out_specs, check_vma=False)
```

time: 599 us -> 150 us (0.25)
  blocking collectives: 320 us -> 0 us
  waiting for transfers between devices: 191 us -> 0 us
  Pallas kernels: 0 us -> 138 us
  local copies, waits for them, and re-layouts: 41.7 us -> 4.11 us
  matrix products: 24.3 us -> 1.43 us
  between operations: 13.6 us -> 0.12 us
    all_to_all x2 -> x0, blocking collectives: 290 us -> none  [the longest x1 146 us: local(): lax.all_to_all(dispatched, 'seq', split_axis=0, concat_axis=2, tiled=True)]
    reduce_scatter x1 -> x0, waiting for transfers between devices: 145 us -> none  [local(): lax.psum_scatter(returned.astype(jnp.float32).astype(jnp.bfloat16), 'teac...]
    pallas_call x0 -> x1, Pallas kernels: none -> 138 us  [local(): pl.pallas_call(kernel, out_shape=jax.ShapeDtypeStruct((tok_dev, SUB, LANE...]
    all_gather x1 -> x0, waiting for transfers between devices: 45.8 us -> none  [local(): lax.all_gather(normed, 'teacher', axis=0, tiled=True)]
    all_gather x1 -> x0, blocking collectives: 29.3 us -> none  [local(): lax.all_gather(target, 'teacher', axis=0, tiled=True)]
    dot_general x3 -> x1, matrix products: 24 us -> 0.2 us  [plan_routes(): jnp.dot(earlier.astype(jnp.bfloat16), hits.astype(jnp.bfloat16), preferre...]
    all_to_all x3 -> x0, local copies, waits for them, and re-layouts: 21.1 us -> none  [the longest x1 13.9 us: local(): lax.all_to_all(dispatched, 'seq', split_axis=0, concat_axis=2, tiled=True)]
    reshape x2 -> x0, local copies, waits for them, and re-layouts: 6.37 us -> none  [the longest x1 6.23 us: local(): expert_mlp(shaped, gate_weight, up_weight, down_weight)]
  transfers between devices with their start and end apart: 2 -> 0, of which waited for: 2 -> 0; matrix products, arithmetic and copies ran while one was open for 1% -> 0% of each run, Pallas kernels for 0% -> 0%
where the time goes in v1:
time: 150 us
  Pallas kernels  138 us (92%)
  other arithmetic  6.5 us (4%)
  local copies, waits for them, and re-layouts  4.11 us (3%)
    pallas_call x1, Pallas kernels, local(): pl.pallas_call(kernel, out_shape=jax.ShapeDtypeStruct((tok_dev, SUB, LANE...  138 us
    unnamed x10, local copies, waits for them, and re-layouts  3.63 us

profile of v1, /device:TPU:1, one launch (start us, length us, event | category | flops | bytes accessed | tf_op | source)
XLA Modules:
  0.0 150.0 jit_solution(10012492462800324229)
XLA Ops:
  0.0 0.0 copy-start
  0.0 0.0 copy-start.1
  0.0 1.2 fusion
  1.3 0.8 select_reduce_fusion.3
  2.1 0.8 fusion.5
  2.9 0.2 convolution_convert_fusion
  3.1 0.9 select_reduce_fusion.2
  4.0 0.7 add_select_fusion
  4.7 0.1 copy.14
  4.8 0.1 eq.50
  4.9 0.1 select_reduce_fusion.table_ref
  5.0 0.0 copy-done
  5.0 1.2 fusion.3
  6.3 0.8 select_reduce_fusion.1
  7.2 0.1 copy.15
  7.3 0.2 reshape.77.weight_ref
  7.4 1.1 fusion.2
  8.6 0.0 copy-done.1
  8.6 0.0 copy-start.2
  8.6 1.4 copy-done.2
  10.0 0.0 copy-start.3
  10.0 1.4 copy-done.3
  11.4 137.8 %shard_map.73 = bf16[64,16,128]{2,1,0:T(8,128)(2,1)S(1)} custom-call(s32[192]{0:T(256)S(1)} %select_reduce_fusion.table_ref, s32[128]{0:T(128)S(1)} %broadcast_maximum_fusion.target_ref, f32[128]{0:T(128)S(1)} %reshape.77.weight_ref, bf16[64,16,128]{2,1,0:T(8,128)(2,1)S(1)} %bitcast.8, bf16[2,192,2048]{2,1,0:T(8,128)(2,1)S(1)} %copy-done.1, ...), custom_call_target="tpu_custom_call" | custom-call | tf_op jit(solution)/shard_map/pallas_call | solution.py:295
  149.2 0.8 copy.19
  (8 shorter events, 0.1 us)
Async XLA Ops:
  0.0 5.0 %copy-start = (bf16[2048,64]{0,1:T(8,128)(2,1)S(1)}, bf16[2048,64]{0,1:T(8,128)(2,1)}, u32[]{:S(2)}) copy-start(bf16[2048,64]{0,1:T(8,128)(2,1)} %param.8) | copy-start | bytes 786436
  0.0 8.6 %copy-start.1 = (bf16[2,192,2048]{2,1,0:T(8,128)(2,1)S(1)}, bf16[2,192,2048]{2,1,0:T(8,128)(2,1)}, u32[]{:S(2)}) copy-start(bf16[2,192,2048]{2,1,0:T(8,128)(2,1)} %gate_ref.1) | copy-start | bytes 4718596
  8.6 1.4 copy-start.2
  10.0 1.4 copy-start.3

commit v2 on v0

v2 whole, which is shorter than its diff:
```python
import jax
import jax.numpy as jnp
from jax import lax
from jax.experimental import pallas as pl
from jax.experimental.pallas import tpu as pltpu
from jax.sharding import PartitionSpec as P

MESH = pl.DeviceIdType.MESH
NX, NY, NZ, NLO = 4, 4, 8, 4
PLANE = NX * NY
LANE = 128
SUB = 16
CHUNKS = 4
ORDER = (1, 3, 2)


def device(x, y, z, core):
    return ((z // NLO) * NX + x, (y * NLO + z % NLO) * 2 + core)


def split(values, by):
    if by == 16:
        whole = lax.shift_right_logical(values, 4)
    else:
        whole = lax.shift_right_logical(values * 171, {3: 9, 12: 11, 48: 13}[by])
    return whole, values - whole * by


def slot_columns(shape, per_place, cap):
    place, left = split(lax.broadcasted_iota(jnp.int32, shape, 1), per_place)
    z_lo, rank = split(left, cap)
    y, x = lax.shift_right_logical(place, 2), place & (NX - 1)
    expert = jnp.where(left < NLO * cap, (y * NLO + z_lo) * NX + x, -1)
    return expert, rank


def copy(src, dst, sem):
    return pltpu.make_async_copy(src, dst, sem)


def push(src, dst, send_sem, recv_sem, to):
    pltpu.make_async_remote_copy(
        src_ref=src, dst_ref=dst, send_sem=send_sem, recv_sem=recv_sem,
        device_id=to, device_id_type=MESH,
    ).start()


def take(ref, sem):
    pltpu.make_async_copy(ref, ref, sem).wait()


def kernel(
    lengths_ref, tok_ref, router_ref, routing_ref, gate_ref, up_ref, down_ref, out_ref,
    normed, mix_hi, mix_lo, order, gather, send1, plane_in, recv, rows_in, gate_up, down,
    hidden, sorted_hidden, stage, rsend, z_back, xsend, back,
    g_send, g_recv, gf_send, gf_recv, d_send, d_recv, df_send, df_recv,
    p_send, p_recv, z_send, z_recv, rz_send, rz_recv, rp_send, rp_recv,
):
    f32, bf16 = jnp.float32, jnp.bfloat16
    teacher, seq = lax.axis_index("teacher"), lax.axis_index("seq")
    x, z_hi = teacher % NX, teacher // NX
    core, z_lo, y = seq % 2, (seq // 2) % NLO, seq // (2 * NLO)
    z = z_hi * NLO + z_lo
    here = y * NX + x
    sibling = device(x, y, z, 1 - core)
    tokens, width = tok_ref.shape
    depth = gate_ref.shape[1]
    half = depth // 2
    cap = send1.shape[2]
    wide = width // CHUNKS
    rows = rows_in.shape[0]
    group = rows // NY
    per_z = rows // NZ

    barrier = pltpu.get_barrier_semaphore()

    def greet(to):
        pl.semaphore_signal(barrier, inc=1, device_id=to, device_id_type=MESH)

    @pl.loop(0, NX)
    def _(px):
        greet(device(px, y, z, 1 - core))

    @pl.loop(1, PLANE)
    def _(i):
        at = (here + i) % PLANE
        greet(device(at % NX, at // NX, z, core))

    @pl.loop(1, NZ)
    def _(i):
        greet(device(x, y, (z + i) % NZ, core))

    pl.semaphore_wait(barrier, NX + PLANE - 1 + NZ - 1)

    def send_gate_up(i, m, part):
        ref = (gate_ref, up_ref)[m]
        goal = 2 * core + i
        at = pl.ds(part * half, half)

        @pl.when(goal != x)
        def _():
            push(
                ref.at[i, at, :], gate_up.at[x, m, at, :], g_send, g_recv.at[x],
                device(goal, y, z, part),
            )

        @pl.when(goal == x)
        def _():
            copy(ref.at[i, at, :], gate_up.at[x, m, at, :], g_recv.at[x]).start()
            push(ref.at[i, at, :], gate_up.at[x, m, at, :], g_send, g_recv.at[x], sibling)

    def send_down(i, c, part):
        goal = 2 * core + i
        at, cols = pl.ds(part * half, half), pl.ds(c * wide, wide)

        @pl.when(goal != x)
        def _():
            push(
                down_ref.at[i, at, cols], down.at[x, at, cols], d_send, d_recv.at[x, c],
                device(goal, y, z, part),
            )

        @pl.when(goal == x)
        def _():
            copy(down_ref.at[i, at, cols], down.at[x, at, cols], d_recv.at[x, c]).start()
            push(down_ref.at[i, at, cols], down.at[x, at, cols], d_send, d_recv.at[x, c], sibling)

    for i in range(2):
        send_gate_up(i, 0, 0)

    values = tok_ref[...].astype(f32)
    scale = lax.rsqrt(jnp.mean(values * values, axis=-1, keepdims=True) + 1e-06)
    normed[...] = (values * scale).astype(bf16)
    block = teacher * (2 * NLO * NY) + seq
    first = (block % 4) * tokens
    limit = lengths_ref[block // 4]
    live = first + lax.broadcasted_iota(jnp.int32, (tokens, 1), 0) < limit
    name0, name1 = routing_ref[:, 0:1], routing_ref[:, 1:2]
    earlier = (
        lax.broadcasted_iota(jnp.int32, (tokens, tokens), 0)
        > lax.broadcasted_iota(jnp.int32, (tokens, tokens), 1)
    ).astype(f32).astype(bf16)

    def slots(count, per_place):
        expert, rank = slot_columns((tokens, count), per_place, cap)
        named = jnp.logical_or(name0 == expert, name1 == expert)
        hit = jnp.where(jnp.logical_and(named, live), 1.0, 0.0)
        before = jnp.dot(earlier, hit.astype(bf16), preferred_element_type=f32)
        return expert, jnp.where(before == rank.astype(f32), hit, 0.0)

    _, chosen = slots(PLANE * NLO * cap, NLO * cap)
    picked = lax.dot_general(
        chosen.astype(bf16), normed[...], (((0,), (0,)), ((), ())), preferred_element_type=f32
    )
    for k in range(SUB):
        stage[pl.ds(k, PLANE * NLO * cap, stride=SUB), :] = picked[:, k * LANE:(k + 1) * LANE]
    send1[...] = stage[...].astype(bf16).reshape(send1.shape)

    copy(send1.at[here], plane_in.at[here], p_recv.at[y]).start()

    @pl.loop(1, PLANE)
    def _(i):
        at = (here + i) % PLANE
        push(
            send1.at[at], plane_in.at[here], p_send, p_recv.at[y],
            device(at % NX, at // NX, z, core),
        )

    for i in range(2):
        send_gate_up(i, 0, 1)
    for part in range(2):
        for i in range(2):
            send_gate_up(i, 1, part)
    for c in range(CHUNKS):
        for part in range(2):
            for i in range(2):
                send_down(i, c, part)

    logits = jnp.dot(normed[...], router_ref[...], preferred_element_type=f32)
    ids = lax.broadcasted_iota(jnp.int32, logits.shape, 1)

    def score(name):
        return jax.nn.sigmoid(
            jnp.sum(jnp.where(name == ids, logits, 0.0), axis=1, keepdims=True)
        )

    score0, score1 = score(name0), score(name1)
    both = score0 + score1
    expert, used = slots(PLANE * SUB, SUB)
    mix = used * jnp.where(name0 == expert, score0 / both, score1 / both)
    high = mix.astype(bf16)
    mix_hi[...] = high
    mix_lo[...] = (mix - high.astype(f32)).astype(bf16)

    @pl.loop(0, NY)
    def _(i):
        g = (y + i) % NY
        at = pl.ds(g * NX, NX)
        take(plane_in.at[at], p_recv.at[g])
        copy(plane_in.at[at, z_lo], recv.at[g, z], z_recv.at[g]).start()

        @pl.loop(1, NZ)
        def _(j):
            pz = (z + j) % NZ
            push(
                plane_in.at[at, pz % NLO], recv.at[g, z], z_send, z_recv.at[g],
                device(x, y, pz, core),
            )

    i_at, q = split(lax.broadcasted_iota(jnp.int32, (rows, rows), 0), per_z)
    by_y, rest = split(q, NX * cap)
    column = lax.broadcasted_iota(jnp.int32, (rows, rows), 1)
    order[...] = (by_y * group + i_at * (NX * cap) + rest == column).astype(f32).astype(bf16)
    place, left = split(lax.broadcasted_iota(jnp.int32, (PLANE * SUB, rows), 0), SUB)
    from_z, q = split(lax.broadcasted_iota(jnp.int32, (PLANE * SUB, rows), 1), per_z)
    to_place, rank = split(q, cap)
    same = jnp.logical_and(place == to_place, left == (from_z & (NLO - 1)) * cap + rank)
    gather[...] = same.astype(f32).astype(bf16)

    def relayout(i):
        g = (y + i) % NY
        take(recv.at[g], z_recv.at[g])
        part = pl.ds(0, group * SUB)
        stage[part, :] = recv[g].reshape(group * SUB, LANE).astype(f32)
        at = pl.ds(pl.multiple_of(g * group, group), group)
        for k in range(SUB):
            rows_in[at, k * LANE:(k + 1) * LANE] = stage[
                pl.ds(k, group, stride=SUB), :
            ].astype(bf16)

    def first_layer(i):
        g = (y + i) % NY
        at = pl.ds(pl.multiple_of(g * group, group), group)
        block = rows_in[at, :]

        @pl.loop(0, NX)
        def _(s):
            dims = (((1,), (1,)), ((), ()))
            gate = lax.dot_general(block, gate_up[s, 0], dims, preferred_element_type=f32)
            upper = lax.dot_general(block, gate_up[s, 1], dims, preferred_element_type=f32)
            hidden[s, at, :] = (gate / (1.0 + jnp.exp(-gate)) * upper).astype(bf16)

    def gate_half(s, part):
        return gate_up.at[s, :, pl.ds(part * half, half), :]

    def down_half(s, c, part):
        return down.at[s, pl.ds(part * half, half), pl.ds(c * wide, wide)]

    for i in range(2):
        relayout(i)

    for d in ORDER:
        s = (x + d) % NX
        mine = gate_half(s, core)
        take(mine, g_recv.at[s])
        push(mine, mine, gf_send.at[s], gf_recv.at[s], sibling)
    take(gate_up.at[x], g_recv.at[x])
    for d in ORDER:
        s = (x + d) % NX
        take(gate_half(s, 1 - core), gf_recv.at[s])

    for i in range(2):
        first_layer(i)
    for i in range(2, 4):
        relayout(i)
    for i in range(2, 4):
        first_layer(i)

    @pl.loop(0, NX)
    def _(s):
        sorted_hidden[s] = jnp.dot(
            order[...], hidden[s], preferred_element_type=f32
        ).astype(bf16)

    for c in range(CHUNKS):
        for d in ORDER:
            s = (x + d) % NX
            mine = down_half(s, c, core)
            take(mine, d_recv.at[s, c])
            push(mine, mine, df_send.at[s, c], df_recv.at[s, c], sibling)
        cols = pl.ds(c * wide, wide)
        take(down.at[x, :, cols], d_recv.at[x, c])
        for d in ORDER:
            s = (x + d) % NX
            take(down_half(s, c, 1 - core), df_recv.at[s, c])

        @pl.loop(0, rows // 128)
        def _(b):
            at = pl.ds(pl.multiple_of(b * 128, 128), 128)
            total = jnp.zeros((128, wide), f32)
            for s in range(NX):
                total += jnp.dot(
                    sorted_hidden[s, at, :], down[s, :, c * wide:(c + 1) * wide],
                    preferred_element_type=f32,
                )
            rsend[c, at, :] = total.astype(bf16)

        def mine_of(pz):
            return rsend.at[c, pl.ds(pl.multiple_of(pz * per_z, per_z), per_z), :]

        copy(mine_of(z), z_back.at[c, pl.ds(pl.multiple_of(z * per_z, per_z), per_z), :],
             rz_recv.at[c]).start()

        @pl.loop(1, NZ)
        def _(j):
            pz = (z + j) % NZ
            push(
                mine_of(pz),
                z_back.at[c, pl.ds(pl.multiple_of(z * per_z, per_z), per_z), :],
                rz_send, rz_recv.at[c], device(x, y, pz, core),
            )

    def finish(c):
        take(back.at[c], rp_recv.at[c])
        total = jnp.dot(mix_hi[...], back[c], preferred_element_type=f32)
        total += jnp.dot(mix_lo[...], back[c], preferred_element_type=f32)
        out_ref[:, c * wide:(c + 1) * wide] = total.astype(bf16)

    for c in range(CHUNKS):
        take(z_back.at[c], rz_recv.at[c])
        xsend[c] = jnp.dot(gather[...], z_back[c], preferred_element_type=f32).astype(bf16)
        landing = back.at[c, pl.ds(pl.multiple_of(here * SUB, SUB), SUB), :]
        copy(
            xsend.at[c, pl.ds(pl.multiple_of(here * SUB, SUB), SUB), :], landing, rp_recv.at[c]
        ).start()

        @pl.loop(1, PLANE)
        def _(i):
            at = (here + i) % PLANE
            push(
                xsend.at[c, pl.ds(pl.multiple_of(at * SUB, SUB), SUB), :], landing,
                rp_send, rp_recv.at[c], device(at % NX, at // NX, z, core),
            )

        if c > 0:
            finish(c - 1)
    finish(CHUNKS - 1)

    take(plane_in.at[pl.ds(0, PLANE - 1)], p_send)
    take(recv.at[:, pl.ds(0, NZ - 1)], z_send)
    take(z_back.at[:, pl.ds(0, rows - per_z), :], rz_send)
    take(back.at[:, pl.ds(0, (PLANE - 1) * SUB), :], rp_send)
    take(gate_up.at[pl.ds(0, 2)], g_send)
    take(down.at[pl.ds(0, 2)], d_send)
    for d in ORDER:
        s = (x + d) % NX
        take(gate_half(s, core), gf_send.at[s])
        for c in range(CHUNKS):
            take(down_half(s, c, core), df_send.at[s, c])


def local(tokens, router_weight, gate_weight, up_weight, down_weight, routing, lengths):
    tok_dev, width = tokens.shape
    top_count = routing.shape[1]
    experts = gate_weight.shape[0] * lax.axis_size("seq")
    depth = gate_weight.shape[1]
    cap = max(2, tok_dev * top_count // experts + 1)
    rows = PLANE * NZ * cap
    wide = width // CHUNKS
    smem = pl.BlockSpec(memory_space=pltpu.SMEM)
    vmem = pl.BlockSpec(memory_space=pltpu.VMEM)
    hbm = pl.BlockSpec(memory_space=pl.ANY)
    sem = pltpu.SemaphoreType.DMA
    bf16 = jnp.bfloat16
    return pl.pallas_call(
        kernel,
        out_shape=jax.ShapeDtypeStruct((tok_dev, width), bf16),
        in_specs=[smem, vmem, vmem, vmem, hbm, hbm, hbm],
        out_specs=vmem,
        scratch_shapes=[
            pltpu.VMEM((tok_dev, width), bf16),
            pltpu.VMEM((tok_dev, PLANE * SUB), bf16),
            pltpu.VMEM((tok_dev, PLANE * SUB), bf16),
            pltpu.VMEM((rows, rows), bf16),
            pltpu.VMEM((PLANE * SUB, rows), bf16),
            pltpu.VMEM((PLANE, NLO, cap, SUB, LANE), bf16),
            pltpu.VMEM((PLANE, NLO, cap, SUB, LANE), bf16),
            pltpu.VMEM((NY, NZ, NX, cap, SUB, LANE), bf16),
            pltpu.VMEM((rows, width), bf16),
            pltpu.VMEM((NX, 2, depth, width), bf16),
            pltpu.VMEM((NX, depth, width), bf16),
            pltpu.VMEM((NX, rows, depth), bf16),
            pltpu.VMEM((NX, rows, depth), bf16),
            pltpu.VMEM((PLANE * NLO * cap * SUB, LANE), jnp.float32),
            pltpu.VMEM((CHUNKS, rows, wide), bf16),
            pltpu.VMEM((CHUNKS, rows, wide), bf16),
            pltpu.VMEM((CHUNKS, PLANE * SUB, wide), bf16),
            pltpu.VMEM((CHUNKS, PLANE * SUB, wide), bf16),
            sem, sem((NX,)), sem((NX,)), sem((NX,)),
            sem, sem((NX, CHUNKS)), sem((NX, CHUNKS)), sem((NX, CHUNKS)),
            sem, sem((NY,)), sem, sem((NY,)),
            sem, sem((CHUNKS,)), sem, sem((CHUNKS,)),
        ],
        compiler_params=pltpu.CompilerParams(
            collective_id=0, has_side_effects=True, vmem_limit_bytes=48 * 1024 * 1024
        ),
    )(lengths, tokens, router_weight, routing, gate_weight, up_weight, down_weight)


def solution(mesh):
    in_specs = (
        P(("teacher", "seq"), None),
        P(),
        P("seq", "teacher", None),
        P("seq", "teacher", None),
        P("seq", "teacher", None),
        P(("teacher", "seq"), None),
        P(),
    )
    out_specs = P(("teacher", "seq"), None)
    return jax.shard_map(local, mesh=mesh, in_specs=in_specs, out_specs=out_specs, check_vma=False)
```

time: 599 us -> 126 us (0.21)
  blocking collectives: 320 us -> 0 us
  waiting for transfers between devices: 191 us -> 0 us
  Pallas kernels: 0 us -> 117 us
  local copies, waits for them, and re-layouts: 41.7 us -> 8.52 us
  matrix products: 24.3 us -> 0 us
  between operations: 13.6 us -> 0.03 us
  other arithmetic: 8.46 us -> 0 us
    all_to_all x2 -> x0, blocking collectives: 290 us -> none  [the longest x1 146 us: local(): lax.all_to_all(dispatched, 'seq', split_axis=0, concat_axis=2, tiled=True)]
    reduce_scatter x1 -> x0, waiting for transfers between devices: 145 us -> none  [local(): lax.psum_scatter(returned.astype(jnp.float32).astype(jnp.bfloat16), 'teac...]
    pallas_call x0 -> x1, Pallas kernels: none -> 117 us  [local(): pl.pallas_call(kernel, out_shape=jax.ShapeDtypeStruct((tok_dev, width), b...]
    all_gather x1 -> x0, waiting for transfers between devices: 45.8 us -> none  [local(): lax.all_gather(normed, 'teacher', axis=0, tiled=True)]
    all_gather x1 -> x0, blocking collectives: 29.3 us -> none  [local(): lax.all_gather(target, 'teacher', axis=0, tiled=True)]
    dot_general x4 -> x0, matrix products: 24.3 us -> none  [the longest x1 15.3 us: expert_mlp(): jnp.einsum('erf,efd->erd', hidden, down_weight, preferred_element_type=jn...]
    all_to_all x3 -> x0, local copies, waits for them, and re-layouts: 21.1 us -> none  [the longest x1 13.9 us: local(): lax.all_to_all(dispatched, 'seq', split_axis=0, concat_axis=2, tiled=True)]
    reshape x2 -> x0, local copies, waits for them, and re-layouts: 6.37 us -> none  [the longest x1 6.23 us: local(): expert_mlp(shaped, gate_weight, up_weight, down_weight)]
  transfers between devices with their start and end apart: 2 -> 0, of which waited for: 2 -> 0; matrix products, arithmetic and copies ran while one was open for 1% -> 0% of each run, Pallas kernels for 0% -> 0%
where the time goes in v2:
time: 126 us
  Pallas kernels  117 us (93%)
  local copies, waits for them, and re-layouts  8.52 us (7%)
    pallas_call x1, Pallas kernels, local(): pl.pallas_call(kernel, out_shape=jax.ShapeDtypeStruct((tok_dev, width), b...  117 us
    unnamed x13, local copies, waits for them, and re-layouts  8.52 us

profile of v2, /device:TPU:1, one launch (start us, length us, event | category | flops | bytes accessed | tf_op | source)
XLA Modules:
  0.0 125.8 jit_solution(14023731957535889559)
XLA Ops:
  0.0 0.8 copy.9.routing_ref
  0.8 1.2 copy.8.router_ref
  2.0 0.0 copy-start
  2.0 1.4 %copy-done = bf16[2,192,2048]{2,1,0:T(8,128)(2,1)S(1)} copy-done((bf16[2,192,2048]{2,1,0:T(8,128)(2,1)S(1)}, bf16[2,192,2048]{2,1,0:T(8,128)(2,1)}, u32[]{:S(2)}) %copy-start) | copy-done | bytes 1572888
  3.4 0.0 copy-start.1
  3.4 1.4 %copy-done.1 = bf16[2,192,2048]{2,1,0:T(8,128)(2,1)S(1)} copy-done((bf16[2,192,2048]{2,1,0:T(8,128)(2,1)S(1)}, bf16[2,192,2048]{2,1,0:T(8,128)(2,1)}, u32[]{:S(2)}) %copy-start.1) | copy-done | bytes 1572888
  4.8 0.0 copy-start.2
  4.8 1.4 %copy-done.2 = bf16[2,192,2048]{2,1,0:T(8,128)(2,1)S(1)} copy-done((bf16[2,192,2048]{2,1,0:T(8,128)(2,1)S(1)}, bf16[2,192,2048]{2,1,0:T(8,128)(2,1)}, u32[]{:S(2)}) %copy-start.2) | copy-done | bytes 1572888
  6.2 0.0 copy-start.3
  6.2 0.9 copy-done.3
  7.2 0.0 copy-start.4
  7.2 0.7 copy-done.4
  7.8 117.3 %shard_map.73 = bf16[64,2048]{1,0:T(8,128)(2,1)S(1)} custom-call(s32[64]{0:T(128)S(1)} %copy-done.4, bf16[64,2048]{1,0:T(8,128)(2,1)S(1)} %copy-done.3, bf16[2048,64]{1,0:T(8,128)(2,1)S(1)} %copy.8.router_ref, s32[64,2]{1,0:T(8,128)S(1)} %copy.9.routing_ref, bf16[2,192,2048]{2,1,0:T(8,128)(2,1)S(1)} %copy-done, bf16[2,192,2048]{2,1,0:T(8,128)(2,1)S(1)} %copy-done.1, ...), custom_call_target="tpu_custom_call" | custom-call | tf_op jit(solution)/shard_map/pallas_call | solution.py:365
  125.1 0.7 copy.11
Async XLA Ops:
  2.0 1.4 %copy-start = (bf16[2,192,2048]{2,1,0:T(8,128)(2,1)S(1)}, bf16[2,192,2048]{2,1,0:T(8,128)(2,1)}, u32[]{:S(2)}) copy-start(bf16[2,192,2048]{2,1,0:T(8,128)(2,1)} %gate_ref.1) | copy-start | bytes 4718596
  3.4 1.4 %copy-start.1 = (bf16[2,192,2048]{2,1,0:T(8,128)(2,1)S(1)}, bf16[2,192,2048]{2,1,0:T(8,128)(2,1)}, u32[]{:S(2)}) copy-start(bf16[2,192,2048]{2,1,0:T(8,128)(2,1)} %up_ref.1) | copy-start | bytes 4718596
  4.8 1.4 %copy-start.2 = (bf16[2,192,2048]{2,1,0:T(8,128)(2,1)S(1)}, bf16[2,192,2048]{2,1,0:T(8,128)(2,1)}, u32[]{:S(2)}) copy-start(bf16[2,192,2048]{2,1,0:T(8,128)(2,1)} %down_ref.1) | copy-start | bytes 4718596
  6.2 0.9 copy-start.3
  7.2 0.7 copy-start.4

commit v3 on v2

--- a/solution.py
+++ b/solution.py
@@ -50,11 +50,11 @@
 
 
 def kernel(
-    lengths_ref, tok_ref, router_ref, routing_ref, gate_ref, up_ref, down_ref, out_ref,
-    normed, mix_hi, mix_lo, order, gather, send1, plane_in, recv, rows_in, gate_up, down,
+    lengths_hbm, tok_hbm, router_hbm, routing_hbm, gate_ref, up_ref, down_ref, out_ref,
+    lengths_ref, tok_ref, router_ref, routing_ref, normed, mix_hi, mix_lo, order, gather, send1, plane_in, recv, rows_in, gate_up, down,
     hidden, sorted_hidden, stage, rsend, z_back, xsend, back,
     g_send, g_recv, gf_send, gf_recv, d_send, d_recv, df_send, df_recv,
-    p_send, p_recv, z_send, z_recv, rz_send, rz_recv, rp_send, rp_recv,
+    p_send, p_recv, z_send, z_recv, rz_send, rz_recv, rp_send, rp_recv, in_sem,
 ):
     f32, bf16 = jnp.float32, jnp.bfloat16
     teacher, seq = lax.axis_index("teacher"), lax.axis_index("seq")
@@ -72,6 +72,13 @@
     group = rows // NY
     per_z = rows // NZ
 
+    own = (
+        (tok_hbm, tok_ref), (lengths_hbm, lengths_ref), (routing_hbm, routing_ref),
+        (router_hbm, router_ref),
+    )
+    for n, (src, dst) in enumerate(own):
+        copy(src, dst, in_sem.at[n]).start()
+
     barrier = pltpu.get_barrier_semaphore()
 
     def greet(to):
@@ -89,8 +96,6 @@
     @pl.loop(1, NZ)
     def _(i):
         greet(device(x, y, (z + i) % NZ, core))
-
-    pl.semaphore_wait(barrier, NX + PLANE - 1 + NZ - 1)
 
     def send_gate_up(i, m, part):
         ref = (gate_ref, up_ref)[m]
@@ -125,9 +130,8 @@
             copy(down_ref.at[i, at, cols], down.at[x, at, cols], d_recv.at[x, c]).start()
             push(down_ref.at[i, at, cols], down.at[x, at, cols], d_send, d_recv.at[x, c], sibling)
 
-    for i in range(2):
-        send_gate_up(i, 0, 0)
-
+    for n in range(3):
+        copy(*own[n], in_sem.at[n]).wait()
     values = tok_ref[...].astype(f32)
     scale = lax.rsqrt(jnp.mean(values * values, axis=-1, keepdims=True) + 1e-06)
     normed[...] = (values * scale).astype(bf16)
@@ -135,10 +139,17 @@
     first = (block % 4) * tokens
     limit = lengths_ref[block // 4]
     live = first + lax.broadcasted_iota(jnp.int32, (tokens, 1), 0) < limit
-    name0, name1 = routing_ref[:, 0:1], routing_ref[:, 1:2]
+    square = (tokens, tokens)
+    diagonal = lax.broadcasted_iota(jnp.int32, square, 0) == lax.broadcasted_iota(
+        jnp.int32, square, 1
+    )
+
+    def upright(row):
+        return jnp.sum(jnp.where(diagonal, row, 0), axis=1, keepdims=True)
+
+    name0, name1 = upright(routing_ref[0:1, :]), upright(routing_ref[1:2, :])
     earlier = (
-        lax.broadcasted_iota(jnp.int32, (tokens, tokens), 0)
-        > lax.broadcasted_iota(jnp.int32, (tokens, tokens), 1)
+        lax.broadcasted_iota(jnp.int32, square, 0) > lax.broadcasted_iota(jnp.int32, square, 1)
     ).astype(f32).astype(bf16)
 
     def slots(count, per_place):
@@ -156,27 +167,30 @@
         stage[pl.ds(k, PLANE * NLO * cap, stride=SUB), :] = picked[:, k * LANE:(k + 1) * LANE]
     send1[...] = stage[...].astype(bf16).reshape(send1.shape)
 
+    pl.semaphore_wait(barrier, NX + PLANE - 1 + NZ - 1)
     copy(send1.at[here], plane_in.at[here], p_recv.at[y]).start()
 
     @pl.loop(1, PLANE)
     def _(i):
-        at = (here + i) % PLANE
+        px, py = (x + i) % NX, (y + i // NX) % NY
         push(
-            send1.at[at], plane_in.at[here], p_send, p_recv.at[y],
-            device(at % NX, at // NX, z, core),
+            send1.at[py * NX + px], plane_in.at[here], p_send, p_recv.at[y],
+            device(px, py, z, core),
         )
 
-    for i in range(2):
-        send_gate_up(i, 0, 1)
-    for part in range(2):
-        for i in range(2):
-            send_gate_up(i, 1, part)
+    for m in range(2):
+        for part in range(2):
+            for i in range(2):
+                send_gate_up(i, m, part)
     for c in range(CHUNKS):
         for part in range(2):
             for i in range(2):
                 send_down(i, c, part)
 
-    logits = jnp.dot(normed[...], router_ref[...], preferred_element_type=f32)
+    copy(*own[3], in_sem.at[3]).wait()
+    logits = lax.dot_general(
+        normed[...], router_ref[...], (((1,), (1,)), ((), ())), preferred_element_type=f32
+    )
     ids = lax.broadcasted_iota(jnp.int32, logits.shape, 1)
 
     def score(name):
@@ -194,7 +208,7 @@
 
     @pl.loop(0, NY)
     def _(i):
-        g = (y + i) % NY
+        g = (y + NY - i) % NY
         at = pl.ds(g * NX, NX)
         take(plane_in.at[at], p_recv.at[g])
         copy(plane_in.at[at, z_lo], recv.at[g, z], z_recv.at[g]).start()
@@ -210,7 +224,8 @@
     i_at, q = split(lax.broadcasted_iota(jnp.int32, (rows, rows), 0), per_z)
     by_y, rest = split(q, NX * cap)
     column = lax.broadcasted_iota(jnp.int32, (rows, rows), 1)
-    order[...] = (by_y * group + i_at * (NX * cap) + rest == column).astype(f32).astype(bf16)
+    turn = (y + NY - by_y) & (NY - 1)
+    order[...] = (turn * group + i_at * (NX * cap) + rest == column).astype(f32).astype(bf16)
     place, left = split(lax.broadcasted_iota(jnp.int32, (PLANE * SUB, rows), 0), SUB)
     from_z, q = split(lax.broadcasted_iota(jnp.int32, (PLANE * SUB, rows), 1), per_z)
     to_place, rank = split(q, cap)
@@ -218,27 +233,21 @@
     gather[...] = same.astype(f32).astype(bf16)
 
     def relayout(i):
-        g = (y + i) % NY
+        g = (y + NY - i) % NY
         take(recv.at[g], z_recv.at[g])
         part = pl.ds(0, group * SUB)
         stage[part, :] = recv[g].reshape(group * SUB, LANE).astype(f32)
-        at = pl.ds(pl.multiple_of(g * group, group), group)
+        at = slice(i * group, (i + 1) * group)
         for k in range(SUB):
             rows_in[at, k * LANE:(k + 1) * LANE] = stage[
                 pl.ds(k, group, stride=SUB), :
             ].astype(bf16)
 
-    def first_layer(i):
-        g = (y + i) % NY
-        at = pl.ds(pl.multiple_of(g * group, group), group)
-        block = rows_in[at, :]
-
-        @pl.loop(0, NX)
-        def _(s):
-            dims = (((1,), (1,)), ((), ()))
-            gate = lax.dot_general(block, gate_up[s, 0], dims, preferred_element_type=f32)
-            upper = lax.dot_general(block, gate_up[s, 1], dims, preferred_element_type=f32)
-            hidden[s, at, :] = (gate / (1.0 + jnp.exp(-gate)) * upper).astype(bf16)
+    def first_layer(s, at):
+        dims = (((1,), (1,)), ((), ()))
+        gate = lax.dot_general(rows_in[at, :], gate_up[s, 0], dims, preferred_element_type=f32)
+        upper = lax.dot_general(rows_in[at, :], gate_up[s, 1], dims, preferred_element_type=f32)
+        hidden[s, at, :] = (gate / (1.0 + jnp.exp(-gate)) * upper).astype(bf16)
 
     def gate_half(s, part):
         return gate_up.at[s, :, pl.ds(part * half, half), :]
@@ -246,25 +255,25 @@
     def down_half(s, c, part):
         return down.at[s, pl.ds(part * half, half), pl.ds(c * wide, wide)]
 
-    for i in range(2):
-        relayout(i)
-
+    relayout(0)
+    relayout(1)
+    take(gate_up.at[x], g_recv.at[x])
+    first_layer(x, slice(0, 2 * group))
     for d in ORDER:
         s = (x + d) % NX
         mine = gate_half(s, core)
         take(mine, g_recv.at[s])
         push(mine, mine, gf_send.at[s], gf_recv.at[s], sibling)
-    take(gate_up.at[x], g_recv.at[x])
+    relayout(2)
+    relayout(3)
+    first_layer(x, slice(2 * group, 4 * group))
     for d in ORDER:
         s = (x + d) % NX
         take(gate_half(s, 1 - core), gf_recv.at[s])
 
-    for i in range(2):
-        first_layer(i)
-    for i in range(2, 4):
-        relayout(i)
-    for i in range(2, 4):
-        first_layer(i)
+    @pl.loop(1, NX)
+    def _(d):
+        first_layer((x + d) % NX, slice(0, rows))
 
     @pl.loop(0, NX)
     def _(s):
@@ -357,17 +366,20 @@
     cap = max(2, tok_dev * top_count // experts + 1)
     rows = PLANE * NZ * cap
     wide = width // CHUNKS
-    smem = pl.BlockSpec(memory_space=pltpu.SMEM)
     vmem = pl.BlockSpec(memory_space=pltpu.VMEM)
-    hbm = pl.BlockSpec(memory_space=pl.ANY)
+    hbm = pl.BlockSpec(memory_space=pltpu.HBM)
     sem = pltpu.SemaphoreType.DMA
     bf16 = jnp.bfloat16
     return pl.pallas_call(
         kernel,
         out_shape=jax.ShapeDtypeStruct((tok_dev, width), bf16),
-        in_specs=[smem, vmem, vmem, vmem, hbm, hbm, hbm],
+        in_specs=[hbm] * 7,
         out_specs=vmem,
         scratch_shapes=[
+            pltpu.SMEM(lengths.shape, jnp.int32),
+            pltpu.VMEM((tok_dev, width), bf16),
+            pltpu.VMEM((experts, width), bf16),
+            pltpu.VMEM((top_count, tok_dev), jnp.int32),
             pltpu.VMEM((tok_dev, width), bf16),
             pltpu.VMEM((tok_dev, PLANE * SUB), bf16),
             pltpu.VMEM((tok_dev, PLANE * SUB), bf16),
@@ -389,12 +401,12 @@
             sem, sem((NX,)), sem((NX,)), sem((NX,)),
             sem, sem((NX, CHUNKS)), sem((NX, CHUNKS)), sem((NX, CHUNKS)),
             sem, sem((NY,)), sem, sem((NY,)),
-            sem, sem((CHUNKS,)), sem, sem((CHUNKS,)),
+            sem, sem((CHUNKS,)), sem, sem((CHUNKS,)), sem((4,)),
         ],
         compiler_params=pltpu.CompilerParams(
-            collective_id=0, has_side_effects=True, vmem_limit_bytes=48 * 1024 * 1024
+            collective_id=0, has_side_effects=True, vmem_limit_bytes=60 * 1024 * 1024
         ),
-    )(lengths, tokens, router_weight, routing, gate_weight, up_weight, down_weight)
+    )(lengths, tokens, router_weight.T, routing.T, gate_weight, up_weight, down_weight)
 
 
 def solution(mesh):

time: 126 us -> 111 us (0.88)
  Pallas kernels: 117 us -> 109 us
  local copies, waits for them, and re-layouts: 8.52 us -> 1.67 us
    pallas_call x1, Pallas kernels: 117 us -> 109 us  [local(): pl.pallas_call(kernel, out_shape=jax.ShapeDtypeStruct((tok_dev, width), b...]
    unnamed x13 -> x1, local copies, waits for them, and re-layouts: 8.52 us -> 1.67 us
where the time goes in v3:
time: 111 us
  Pallas kernels  109 us (98%)
  local copies, waits for them, and re-layouts  1.67 us (2%)
    pallas_call x1, Pallas kernels, local(): pl.pallas_call(kernel, out_shape=jax.ShapeDtypeStruct((tok_dev, width), b...  109 us

profile of v3, /device:TPU:1, one launch (start us, length us, event | category | flops | bytes accessed | tf_op | source)
XLA Modules:
  0.0 110.9 jit_solution(11691924196051681632)
XLA Ops:
  0.0 109.2 %shard_map.73 = bf16[64,2048]{1,0:T(8,128)(2,1)} custom-call(s32[64]{0:T(128)} %lengths_hbm.1, bf16[64,2048]{1,0:T(8,128)(2,1)} %tok_hbm.1, bf16[64,2048]{1,0:T(8,128)(2,1)} %bitcast.2, s32[2,64]{1,0:T(2,128)} %bitcast.3, bf16[2,192,2048]{2,1,0:T(8,128)(2,1)} %gate_ref.1, bf16[2,192,2048]{2,1,0:T(8,128)(2,1)} %up_ref.1, bf16[2,192,2048]{2,1,0:T(8,128)(2,1)} %down_ref.1), custom_call_target="tpu_custom_call" | custom-call | tf_op jit(solution)/shard_map/pallas_call | solution.py:373
  109.2 1.7 %copy.9 = bf16[64,2048]{1,0:T(8,128)(2,1)} copy(bf16[64,2048]{1,0:T(8,128)(2,1)} %shard_map.73) | data formatting | bytes 524288

commit v4 on v3

--- a/solution.py
+++ b/solution.py
@@ -10,8 +10,10 @@
 PLANE = NX * NY
 LANE = 128
 SUB = 16
-CHUNKS = 4
+CHUNKS = 8
 ORDER = (1, 3, 2)
+LAG = 2
+PIECES = ((0, 0, 2), (1, 0, 1), (1, 1, 1))
 
 
 def device(x, y, z, core):
@@ -52,7 +54,7 @@
 def kernel(
     lengths_hbm, tok_hbm, router_hbm, routing_hbm, gate_ref, up_ref, down_ref, out_ref,
     lengths_ref, tok_ref, router_ref, routing_ref, normed, mix_hi, mix_lo, order, gather, send1, plane_in, recv, rows_in, gate_up, down,
-    hidden, sorted_hidden, stage, rsend, z_back, xsend, back,
+    gates, hidden, sorted_hidden, stage, rsend, z_back, xsend, back,
     g_send, g_recv, gf_send, gf_recv, d_send, d_recv, df_send, df_recv,
     p_send, p_recv, z_send, z_recv, rz_send, rz_recv, rp_send, rp_recv, in_sem,
 ):
@@ -84,35 +86,37 @@
     def greet(to):
         pl.semaphore_signal(barrier, inc=1, device_id=to, device_id_type=MESH)
 
-    @pl.loop(0, NX)
-    def _(px):
-        greet(device(px, y, z, 1 - core))
+    @pl.loop(1, NZ)
+    def _(i):
+        greet(device(x, y, (z + i) % NZ, core))
 
     @pl.loop(1, PLANE)
     def _(i):
         at = (here + i) % PLANE
         greet(device(at % NX, at // NX, z, core))
 
-    @pl.loop(1, NZ)
-    def _(i):
-        greet(device(x, y, (z + i) % NZ, core))
-
-    def send_gate_up(i, m, part):
-        ref = (gate_ref, up_ref)[m]
+    @pl.loop(0, NX)
+    def _(px):
+        greet(device(px, y, z, 1 - core))
+
+    def piece(p, part):
+        m, start, count = PIECES[p]
+        return m, pl.ds(part * half + start * (half // 2), count * (half // 2))
+
+    def send_gate_up(i, p, part):
+        m, at = piece(p, part)
+        src = (gate_ref, up_ref)[m].at[i, at, :]
+        dst = gate_up.at[x, m, at, :]
         goal = 2 * core + i
-        at = pl.ds(part * half, half)
 
         @pl.when(goal != x)
         def _():
-            push(
-                ref.at[i, at, :], gate_up.at[x, m, at, :], g_send, g_recv.at[x],
-                device(goal, y, z, part),
-            )
+            push(src, dst, g_send, g_recv.at[x, p], device(goal, y, z, part))
 
         @pl.when(goal == x)
         def _():
-            copy(ref.at[i, at, :], gate_up.at[x, m, at, :], g_recv.at[x]).start()
-            push(ref.at[i, at, :], gate_up.at[x, m, at, :], g_send, g_recv.at[x], sibling)
+            copy(src, dst, g_recv.at[x, p]).start()
+            push(src, dst, g_send, g_recv.at[x, p], sibling)
 
     def send_down(i, c, part):
         goal = 2 * core + i
@@ -135,6 +139,8 @@
     values = tok_ref[...].astype(f32)
     scale = lax.rsqrt(jnp.mean(values * values, axis=-1, keepdims=True) + 1e-06)
     normed[...] = (values * scale).astype(bf16)
+
+    pl.semaphore_wait(barrier, NX + PLANE - 1 + NZ - 1)
     block = teacher * (2 * NLO * NY) + seq
     first = (block % 4) * tokens
     limit = lengths_ref[block // 4]
@@ -167,7 +173,6 @@
         stage[pl.ds(k, PLANE * NLO * cap, stride=SUB), :] = picked[:, k * LANE:(k + 1) * LANE]
     send1[...] = stage[...].astype(bf16).reshape(send1.shape)
 
-    pl.semaphore_wait(barrier, NX + PLANE - 1 + NZ - 1)
     copy(send1.at[here], plane_in.at[here], p_recv.at[y]).start()
 
     @pl.loop(1, PLANE)
@@ -178,10 +183,10 @@
             device(px, py, z, core),
         )
 
-    for m in range(2):
+    for p in range(len(PIECES)):
         for part in range(2):
             for i in range(2):
-                send_gate_up(i, m, part)
+                send_gate_up(i, p, part)
     for c in range(CHUNKS):
         for part in range(2):
             for i in range(2):
@@ -215,7 +220,7 @@
 
         @pl.loop(1, NZ)
         def _(j):
-            pz = (z + j) % NZ
+            pz = (z + NZ // 2 + (1 - 2 * (j % 2)) * (j // 2)) % NZ
             push(
                 plane_in.at[at, pz % NLO], recv.at[g, z], z_send, z_recv.at[g],
                 device(x, y, pz, core),
@@ -243,43 +248,76 @@
                 pl.ds(k, group, stride=SUB), :
             ].astype(bf16)
 
-    def first_layer(s, at):
-        dims = (((1,), (1,)), ((), ()))
-        gate = lax.dot_general(rows_in[at, :], gate_up[s, 0], dims, preferred_element_type=f32)
-        upper = lax.dot_general(rows_in[at, :], gate_up[s, 1], dims, preferred_element_type=f32)
-        hidden[s, at, :] = (gate / (1.0 + jnp.exp(-gate)) * upper).astype(bf16)
-
-    def gate_half(s, part):
-        return gate_up.at[s, :, pl.ds(part * half, half), :]
-
-    def down_half(s, c, part):
-        return down.at[s, pl.ds(part * half, half), pl.ds(c * wide, wide)]
-
-    relayout(0)
-    relayout(1)
-    take(gate_up.at[x], g_recv.at[x])
-    first_layer(x, slice(0, 2 * group))
-    for d in ORDER:
-        s = (x + d) % NX
-        mine = gate_half(s, core)
-        take(mine, g_recv.at[s])
-        push(mine, mine, gf_send.at[s], gf_recv.at[s], sibling)
-    relayout(2)
-    relayout(3)
-    first_layer(x, slice(2 * group, 4 * group))
-    for d in ORDER:
-        s = (x + d) % NX
-        take(gate_half(s, 1 - core), gf_recv.at[s])
-
-    @pl.loop(1, NX)
-    def _(d):
-        first_layer((x + d) % NX, slice(0, rows))
-
-    @pl.loop(0, NX)
-    def _(s):
+    def times(s, m, at):
+        return lax.dot_general(
+            rows_in[at, :], gate_up[s, m], (((1,), (1,)), ((), ())), preferred_element_type=f32
+        )
+
+    def first_gate(s, at):
+        gates[s, at, :] = times(s, 0, at)
+
+    def first_up(s, at):
+        gate = gates[s, at, :]
+        hidden[s, at, :] = (gate / (1.0 + jnp.exp(-gate)) * times(s, 1, at)).astype(bf16)
+
+    def sort(s):
         sorted_hidden[s] = jnp.dot(
             order[...], hidden[s], preferred_element_type=f32
         ).astype(bf16)
+
+    def down_half(s, c, part):
+        return down.at[s, pl.ds(part * half, half), pl.ds(c * wide, wide)]
+
+    def landed(s, p, part):
+        m, at = piece(p, part)
+        return gate_up.at[s, m, at, :]
+
+    def forward(p):
+        for d in ORDER:
+            s = (x + d) % NX
+            mine = landed(s, p, core)
+            take(mine, g_recv.at[s, p])
+            push(mine, mine, gf_send.at[s, p], gf_recv.at[s, p], sibling)
+
+    def forwarded(p):
+        for d in ORDER:
+            s = (x + d) % NX
+            take(landed(s, p, 1 - core), gf_recv.at[s, p])
+
+    early, late, every = slice(0, 2 * group), slice(2 * group, 4 * group), slice(0, rows)
+    for p, (m, _, count) in enumerate(PIECES):
+        take(gate_up.at[x, m, pl.ds(0, count * half), :], g_recv.at[x, p])
+    relayout(0)
+    relayout(1)
+    first_gate(x, early)
+    first_up(x, early)
+    forward(0)
+    forwarded(0)
+
+    @pl.loop(1, NX)
+    def _(d):
+        first_gate((x + d) % NX, early)
+
+    forward(1)
+    relayout(2)
+    relayout(3)
+    first_gate(x, late)
+    first_up(x, late)
+    sort(x)
+
+    @pl.loop(1, NX)
+    def _(d):
+        first_gate((x + d) % NX, late)
+
+    forward(2)
+    forwarded(1)
+    forwarded(2)
+
+    @pl.loop(1, NX)
+    def _(d):
+        s = (x + d) % NX
+        first_up(s, every)
+        sort(s)
 
     for c in range(CHUNKS):
         for d in ORDER:
@@ -312,7 +350,7 @@
 
         @pl.loop(1, NZ)
         def _(j):
-            pz = (z + j) % NZ
+            pz = (z + NZ // 2 + (1 - 2 * (j % 2)) * (j // 2)) % NZ
             push(
                 mine_of(pz),
                 z_back.at[c, pl.ds(pl.multiple_of(z * per_z, per_z), per_z), :],
@@ -341,9 +379,10 @@
                 rp_send, rp_recv.at[c], device(at % NX, at // NX, z, core),
             )
 
-        if c > 0:
-            finish(c - 1)
-    finish(CHUNKS - 1)
+        if c >= LAG:
+            finish(c - LAG)
+    for c in range(CHUNKS - LAG, CHUNKS):
+        finish(c)
 
     take(plane_in.at[pl.ds(0, PLANE - 1)], p_send)
     take(recv.at[:, pl.ds(0, NZ - 1)], z_send)
@@ -353,7 +392,8 @@
     take(down.at[pl.ds(0, 2)], d_send)
     for d in ORDER:
         s = (x + d) % NX
-        take(gate_half(s, core), gf_send.at[s])
+        for p in range(len(PIECES)):
+            take(landed(s, p, core), gf_send.at[s, p])
         for c in range(CHUNKS):
             take(down_half(s, c, core), df_send.at[s, c])
 
@@ -391,6 +431,7 @@
             pltpu.VMEM((rows, width), bf16),
             pltpu.VMEM((NX, 2, depth, width), bf16),
             pltpu.VMEM((NX, depth, width), bf16),
+            pltpu.VMEM((NX, rows, depth), jnp.float32),
             pltpu.VMEM((NX, rows, depth), bf16),
             pltpu.VMEM((NX, rows, depth), bf16),
             pltpu.VMEM((PLANE * NLO * cap * SUB, LANE), jnp.float32),
@@ -398,7 +439,7 @@
             pltpu.VMEM((CHUNKS, rows, wide), bf16),
             pltpu.VMEM((CHUNKS, PLANE * SUB, wide), bf16),
             pltpu.VMEM((CHUNKS, PLANE * SUB, wide), bf16),
-            sem, sem((NX,)), sem((NX,)), sem((NX,)),
+            sem, *[sem((NX, len(PIECES)))] * 3,
             sem, sem((NX, CHUNKS)), sem((NX, CHUNKS)), sem((NX, CHUNKS)),
             sem, sem((NY,)), sem, sem((NY,)),
             sem, sem((CHUNKS,)), sem, sem((CHUNKS,)), sem((4,)),

time: 111 us -> 108 us (0.973)
  Pallas kernels: 109 us -> 106 us
    pallas_call x1, Pallas kernels: 109 us -> 106 us  [local(): pl.pallas_call(kernel, out_shape=jax.ShapeDtypeStruct((tok_dev, width), b...]
where the time goes in v4:
time: 108 us
  Pallas kernels  106 us (98%)
  local copies, waits for them, and re-layouts  1.67 us (2%)
    pallas_call x1, Pallas kernels, local(): pl.pallas_call(kernel, out_shape=jax.ShapeDtypeStruct((tok_dev, width), b...  106 us

profile of v4, /device:TPU:1, one launch (start us, length us, event | category | flops | bytes accessed | tf_op | source)
XLA Modules:
  0.0 107.8 jit_solution(7766411962039613685)
XLA Ops:
  0.0 106.1 %shard_map.73 = bf16[64,2048]{1,0:T(8,128)(2,1)} custom-call(s32[64]{0:T(128)} %lengths_hbm.1, bf16[64,2048]{1,0:T(8,128)(2,1)} %tok_hbm.1, bf16[64,2048]{1,0:T(8,128)(2,1)} %bitcast.2, s32[2,64]{1,0:T(2,128)} %bitcast.3, bf16[2,192,2048]{2,1,0:T(8,128)(2,1)} %gate_ref.1, bf16[2,192,2048]{2,1,0:T(8,128)(2,1)} %up_ref.1, bf16[2,192,2048]{2,1,0:T(8,128)(2,1)} %down_ref.1), custom_call_target="tpu_custom_call" | custom-call | tf_op jit(solution)/shard_map/pallas_call | solution.py:413
  106.1 1.7 %copy.9 = bf16[64,2048]{1,0:T(8,128)(2,1)} copy(bf16[64,2048]{1,0:T(8,128)(2,1)} %shard_map.73) | data formatting | bytes 524288

commit v5 on v4

--- a/solution.py
+++ b/solution.py
@@ -13,6 +13,7 @@
 CHUNKS = 8
 ORDER = (1, 3, 2)
 LAG = 2
+BEFORE = 2
 PIECES = ((0, 0, 2), (1, 0, 1), (1, 1, 1))
 
 
@@ -187,6 +188,21 @@
         for part in range(2):
             for i in range(2):
                 send_gate_up(i, p, part)
+    @pl.loop(0, NY)
+    def _(i):
+        g = (y + NY - i) % NY
+        at = pl.ds(g * NX, NX)
+        take(plane_in.at[at], p_recv.at[g])
+        copy(plane_in.at[at, z_lo], recv.at[g, z], z_recv.at[g]).start()
+
+        @pl.loop(1, NZ)
+        def _(j):
+            pz = (z + NZ // 2 + (1 - 2 * (j % 2)) * (j // 2)) % NZ
+            push(
+                plane_in.at[at, pz % NLO], recv.at[g, z], z_send, z_recv.at[g],
+                device(x, y, pz, core),
+            )
+
     for c in range(CHUNKS):
         for part in range(2):
             for i in range(2):
@@ -210,21 +226,6 @@
     high = mix.astype(bf16)
     mix_hi[...] = high
     mix_lo[...] = (mix - high.astype(f32)).astype(bf16)
-
-    @pl.loop(0, NY)
-    def _(i):
-        g = (y + NY - i) % NY
-        at = pl.ds(g * NX, NX)
-        take(plane_in.at[at], p_recv.at[g])
-        copy(plane_in.at[at, z_lo], recv.at[g, z], z_recv.at[g]).start()
-
-        @pl.loop(1, NZ)
-        def _(j):
-            pz = (z + NZ // 2 + (1 - 2 * (j % 2)) * (j // 2)) % NZ
-            push(
-                plane_in.at[at, pz % NLO], recv.at[g, z], z_send, z_recv.at[g],
-                device(x, y, pz, core),
-            )
 
     i_at, q = split(lax.broadcasted_iota(jnp.int32, (rows, rows), 0), per_z)
     by_y, rest = split(q, NX * cap)
@@ -313,18 +314,25 @@
     forwarded(1)
     forwarded(2)
 
-    @pl.loop(1, NX)
-    def _(d):
+    def last_up(d):
         s = (x + d) % NX
         first_up(s, every)
         sort(s)
 
-    for c in range(CHUNKS):
+    def forward_down(c):
         for d in ORDER:
             s = (x + d) % NX
             mine = down_half(s, c, core)
             take(mine, d_recv.at[s, c])
             push(mine, mine, df_send.at[s, c], df_recv.at[s, c], sibling)
+
+    pl.loop(1, BEFORE)(last_up)
+    forward_down(0)
+    pl.loop(BEFORE, NX)(last_up)
+
+    for c in range(CHUNKS):
+        if c > 0:
+            forward_down(c)
         cols = pl.ds(c * wide, wide)
         take(down.at[x, :, cols], d_recv.at[x, c])
         for d in ORDER:

time: 108 us -> 106 us (0.981)
  Pallas kernels: 106 us -> 104 us
    pallas_call x1, Pallas kernels: 106 us -> 104 us  [local(): pl.pallas_call(kernel, out_shape=jax.ShapeDtypeStruct((tok_dev, width), b...]
where the time goes in v5:
time: 106 us
  Pallas kernels  104 us (98%)
  local copies, waits for them, and re-layouts  1.67 us (2%)
    pallas_call x1, Pallas kernels, local(): pl.pallas_call(kernel, out_shape=jax.ShapeDtypeStruct((tok_dev, width), b...  104 us

profile of v5, /device:TPU:1, one launch (start us, length us, event | category | flops | bytes accessed | tf_op | source)
XLA Modules:
  0.0 105.6 jit_solution(4558721995716253951)
XLA Ops:
  0.0 104.0 %shard_map.73 = bf16[64,2048]{1,0:T(8,128)(2,1)} custom-call(s32[64]{0:T(128)} %lengths_hbm.1, bf16[64,2048]{1,0:T(8,128)(2,1)} %tok_hbm.1, bf16[64,2048]{1,0:T(8,128)(2,1)} %bitcast.2, s32[2,64]{1,0:T(2,128)} %bitcast.3, bf16[2,192,2048]{2,1,0:T(8,128)(2,1)} %gate_ref.1, bf16[2,192,2048]{2,1,0:T(8,128)(2,1)} %up_ref.1, bf16[2,192,2048]{2,1,0:T(8,128)(2,1)} %down_ref.1), custom_call_target="tpu_custom_call" | custom-call | tf_op jit(solution)/shard_map/pallas_call | solution.py:421
  104.0 1.7 %copy.9 = bf16[64,2048]{1,0:T(8,128)(2,1)} copy(bf16[64,2048]{1,0:T(8,128)(2,1)} %shard_map.73) | data formatting | bytes 524288

commit v6 on v5

--- a/solution.py
+++ b/solution.py
@@ -306,11 +306,12 @@
     first_up(x, late)
     sort(x)
 
+    forward(2)
+
     @pl.loop(1, NX)
     def _(d):
         first_gate((x + d) % NX, late)
 
-    forward(2)
     forwarded(1)
     forwarded(2)
 

time: 106 us -> 106 us (level)
  no operation moved by 1% of the time
where the time goes in v6:
time: 106 us
  Pallas kernels  104 us (98%)
  local copies, waits for them, and re-layouts  1.67 us (2%)
    pallas_call x1, Pallas kernels, local(): pl.pallas_call(kernel, out_shape=jax.ShapeDtypeStruct((tok_dev, width), b...  104 us

profile of v6, /device:TPU:1, one launch (start us, length us, event | category | flops | bytes accessed | tf_op | source)
XLA Modules:
  0.0 106.0 jit_solution(7617530257200864886)
XLA Ops:
  0.0 104.3 %shard_map.73 = bf16[64,2048]{1,0:T(8,128)(2,1)} custom-call(s32[64]{0:T(128)} %lengths_hbm.1, bf16[64,2048]{1,0:T(8,128)(2,1)} %tok_hbm.1, bf16[64,2048]{1,0:T(8,128)(2,1)} %bitcast.2, s32[2,64]{1,0:T(2,128)} %bitcast.3, bf16[2,192,2048]{2,1,0:T(8,128)(2,1)} %gate_ref.1, bf16[2,192,2048]{2,1,0:T(8,128)(2,1)} %up_ref.1, bf16[2,192,2048]{2,1,0:T(8,128)(2,1)} %down_ref.1), custom_call_target="tpu_custom_call" | custom-call | tf_op jit(solution)/shard_map/pallas_call | solution.py:422
  104.3 1.7 %copy.9 = bf16[64,2048]{1,0:T(8,128)(2,1)} copy(bf16[64,2048]{1,0:T(8,128)(2,1)} %shard_map.73) | data formatting | bytes 524288
